TPU v7x, 128 devices: a whole 4x4x4 slice. The times are simulated.
128 devices in a mesh: dp: 32 (over x_hi, z, y), tensor: 4 (over x_lo, core).
Axes of the slice: x: 4 (x_hi: 2, x_lo: 2; x = x_hi * 2 + x_lo), y: 4, z: 4, core: 2. Of those that a mesh axis runs over, the one named last changes fastest.
Arguments:
- tokens: bfloat16 [32768, 640], P(('dp', 'tensor')), may hold values from -6 to 6
- segments: int32 [32, 1024], P('dp'), may hold values from 0 to 2, as said below
- cotangent: bfloat16 [32768, 640], P(('dp', 'tensor')), may hold values from -24 to 24
- w_query: bfloat16 [640, 1024], P('dp', 'tensor'), may hold values from -0.25 to 0.25
- w_keyval: bfloat16 [640, 512], P('dp'), may hold values from -0.25 to 0.25
- w_out: bfloat16 [1024, 640], P('tensor', 'dp'), may hold values from -0.1875 to 0.1875
- w_gate: bfloat16 [640, 2048], P('dp', 'tensor'), may hold values from -0.25 to 0.25
- w_up: bfloat16 [640, 2048], P('dp', 'tensor'), may hold values from -0.25 to 0.25
- w_down: bfloat16 [2048, 640], P('tensor', 'dp'), may hold values from -0.125 to 0.125
- gain_in: float32 [640], replicated, may hold values from 0.25 to 1.75
- gain_post_attn: float32 [640], replicated, may hold values from 0.25 to 1.75
- gain_pre_ff: float32 [640], replicated, may hold values from 0.25 to 1.75
- gain_post_ff: float32 [640], replicated, may hold values from 0.25 to 1.75
- gain_query: float32 [256], replicated, may hold values from 0.25 to 1.75
- gain_key: float32 [256], replicated, may hold values from 0.25 to 1.75
Outputs:
- output: bfloat16 [32768, 640], P(('dp', 'tensor'))
- grad_x: float32 [32768, 640], P(('dp', 'tensor'))
- grad_query: float32 [640, 1024], P('dp', 'tensor')
- grad_keyval: float32 [640, 512], P('dp')
- grad_out: float32 [1024, 640], P('tensor', 'dp')
- grad_gate: float32 [640, 2048], P('dp', 'tensor')
- grad_up: float32 [640, 2048], P('dp', 'tensor')
- grad_down: float32 [2048, 640], P('tensor', 'dp')
- grad_gain_in: float32 [640], replicated
- grad_gain_post_attn: float32 [640], replicated
- grad_gain_pre_ff: float32 [640], replicated
- grad_gain_post_ff: float32 [640], replicated
- grad_gain_query: float32 [256], replicated
- grad_gain_key: float32 [256], replicated
Inputs may be any that keep to these rules, and one draw needn't show every extreme that they name: `segments`: along each row the numbers never fall; each row holds three documents numbered 0, 1, 2, each of one token or more, where document 1 starts within the first 256 tokens and ends within the last 256.
All inputs are finite; a program needn't handle non-finite values.
Results may differ from a plain program's by a relative error of at most 0.024.
Values may be sent and summed in bfloat16 or wider, within the bound.
A program may use at most 128 MiB of HBM per device.

v0:
```python
import jax
import jax.numpy as jnp
from jax import lax
from jax.sharding import PartitionSpec as P

HD = 256
WINDOW = 512
norm_eps = 1e-06
rope_base = 10000.0


def rms_scale(array_in, gain_row):
    return (
        array_in
        * lax.rsqrt(jnp.mean(array_in * array_in, axis=-1, keepdims=True) + norm_eps)
        * gain_row
    )


def rotate_half(array_in):
    half_width = array_in.shape[-1] // 2
    return jnp.concatenate([-array_in[..., half_width:], array_in[..., :half_width]], axis=-1)


def rope_tables(position_ids, head_width):
    inv_freq = rope_base ** (-jnp.arange(0, head_width, 2).astype(jnp.float32) / head_width)
    angles = position_ids.astype(jnp.float32)[:, None] * inv_freq[None, :]
    angles = jnp.concatenate([angles, angles], axis=-1)
    return (jnp.cos(angles), jnp.sin(angles))


def segment_positions(seg_ids):
    row_index = jnp.arange(seg_ids.shape[0], dtype=jnp.int32)
    prev_ids = jnp.concatenate([seg_ids[:1] - 1, seg_ids[:-1]])
    doc_start = lax.cummax(jnp.where(seg_ids != prev_ids, row_index, 0), axis=0)
    return row_index - doc_start


def prepare(raw_rows, gain_row, cos_rows, sin_rows):
    normed = rms_scale(raw_rows, gain_row)
    return normed * cos_rows + rotate_half(normed) * sin_rows


def norm_back(array_in, gain_row, grad_rows):
    _, back_fn = jax.vjp(rms_scale, array_in, gain_row)
    return back_fn(grad_rows)


def gelu_product(gate_rows, up_rows):
    return jax.nn.gelu(gate_rows, approximate=True) * up_rows


def contract_rows(left_rows, right_rows):
    return lax.dot_general(
        left_rows, right_rows, (((0,), (0,)), ((), ())), preferred_element_type=jnp.float32
    )


def project_back(grad_rows, weight_rows):
    return lax.dot_general(
        grad_rows, weight_rows, (((1,), (1,)), ((), ())), preferred_element_type=jnp.float32
    )


def per_device(
    tokens,
    segments,
    cotangent,
    w_query,
    w_keyval,
    w_out,
    w_gate,
    w_up,
    w_down,
    gain_in,
    gain_post_attn,
    gain_pre_ff,
    gain_post_ff,
    gain_query,
    gain_key,
):
    tok_rows = tokens.shape[0]
    seq_rows = tok_rows * lax.axis_size("tensor")
    model_width = tokens.shape[1]
    heads_here = w_query.shape[1] // HD
    seg_ids = segments[0]
    positions = segment_positions(seg_ids)
    cos_rows, sin_rows = rope_tables(positions, HD)
    cos_heads = cos_rows[:, None, :]
    sin_heads = sin_rows[:, None, :]
    score_scale = HD ** (-0.5)
    q_block = min(512, seq_rows)
    key_reach = -(-WINDOW // q_block) * q_block
    key_span = min(seq_rows, q_block + key_reach)
    starts = jnp.arange(seq_rows // q_block, dtype=jnp.int32) * q_block
    x_local = tokens.astype(jnp.float32)
    attn_local = rms_scale(x_local, gain_in).astype(jnp.bfloat16)
    query_full, keyval_full, out_full = (
        lax.all_gather(w_query, "dp", axis=0, tiled=True),
        lax.all_gather(w_keyval, "dp", axis=0, tiled=True),
        lax.all_gather(w_out, "dp", axis=1, tiled=True),
    )
    attn_input = lax.all_gather(attn_local, "tensor", axis=0, tiled=True)
    query_raw = jnp.dot(attn_input, query_full, preferred_element_type=jnp.float32).reshape(
        seq_rows, heads_here, HD
    )
    keyval_raw = jnp.dot(attn_input, keyval_full, preferred_element_type=jnp.float32)
    key_raw = keyval_raw[:, :HD]
    queries = prepare(query_raw, gain_query, cos_heads, sin_heads).astype(jnp.bfloat16)
    key_rows = prepare(key_raw, gain_key, cos_rows, sin_rows).astype(jnp.bfloat16)
    values = keyval_raw[:, HD:].astype(jnp.bfloat16)

    def block_scores(first_row):
        key_start = jnp.clip(first_row - key_reach, 0, seq_rows - key_span)
        query_blk = lax.dynamic_slice_in_dim(queries, first_row, q_block, 0)
        query_index = first_row + jnp.arange(q_block, dtype=jnp.int32)
        key_index = key_start + jnp.arange(key_span, dtype=jnp.int32)
        query_seg = lax.dynamic_slice_in_dim(seg_ids, first_row, q_block, 0)
        offset = query_index[:, None] - key_index[None, :]
        allowed = (query_seg[:, None] == seg_ids[None, :]) & (offset >= 0) & (offset < WINDOW)
        scores = (
            jnp.einsum("qhd,kd->hqk", query_blk, key_rows, preferred_element_type=jnp.float32)
            * score_scale
        )
        scores = jnp.where(allowed[None], scores, -1e30)
        return (scores, query_blk, key_rows, values, key_start)

    def attend(first_row):
        scores, query_blk, key_blk, value_blk, key_start = block_scores(first_row)
        row_max = jnp.max(scores, axis=-1, keepdims=True)
        exp_scores = jnp.exp(scores - row_max)
        exp_sum = jnp.sum(exp_scores, axis=-1, keepdims=True)
        attn_probs = (exp_scores / exp_sum).astype(jnp.bfloat16)
        context_blk = jnp.einsum(
            "hqk,kd->qhd", attn_probs, value_blk, preferred_element_type=jnp.float32
        )
        return (context_blk, (row_max + jnp.log(exp_sum))[..., 0])

    context, log_total = lax.map(attend, starts)
    context_b = context.reshape(seq_rows, heads_here * HD).astype(jnp.bfloat16)
    rows_here = context_b
    attn_proj = lax.psum_scatter(
        jnp.dot(rows_here, out_full, preferred_element_type=jnp.float32),
        "tensor",
        scatter_dimension=0,
        tiled=True,
    )
    mid_rows = x_local + rms_scale(attn_proj, gain_post_attn)
    mlp_local = rms_scale(mid_rows, gain_pre_ff).astype(jnp.bfloat16)
    gate_full, up_full, down_full = (
        lax.all_gather(w_gate, "dp", axis=0, tiled=True),
        lax.all_gather(w_up, "dp", axis=0, tiled=True),
        lax.all_gather(w_down, "dp", axis=1, tiled=True),
    )
    mlp_input = lax.all_gather(mlp_local, "tensor", axis=0, tiled=True)
    gate_rows = jnp.dot(mlp_input, gate_full, preferred_element_type=jnp.float32)
    up_rows = jnp.dot(mlp_input, up_full, preferred_element_type=jnp.float32)
    hidden = gelu_product(gate_rows, up_rows).astype(jnp.bfloat16)
    rows_here = hidden
    mlp_proj = lax.psum_scatter(
        jnp.dot(rows_here, down_full, preferred_element_type=jnp.float32),
        "tensor",
        scatter_dimension=0,
        tiled=True,
    )
    output = (mid_rows + rms_scale(mlp_proj, gain_post_ff)).astype(jnp.bfloat16)
    grad_top = cotangent.astype(jnp.float32)
    d_mlp_f, grad_gain_post_ff = norm_back(mlp_proj, gain_post_ff, grad_top)
    d_mlp_all = lax.all_gather(d_mlp_f.astype(jnp.bfloat16), "tensor", axis=0, tiled=True)
    down_part = contract_rows(hidden, d_mlp_all)
    d_hidden = project_back(d_mlp_all, down_full)
    _, hidden_back = jax.vjp(gelu_product, gate_rows, up_rows)
    d_gate_f, d_up_f = hidden_back(d_hidden)
    d_gate = d_gate_f.astype(jnp.bfloat16)
    d_up = d_up_f.astype(jnp.bfloat16)
    gate_part = contract_rows(mlp_input, d_gate)
    up_part = contract_rows(mlp_input, d_up)
    d_mlp_input = lax.psum_scatter(
        project_back(d_gate, gate_full) + project_back(d_up, up_full),
        "tensor",
        scatter_dimension=0,
        tiled=True,
    )
    grad_gate, grad_up, grad_down = (
        lax.psum_scatter(
            gate_part.astype(jnp.bfloat16), "dp", scatter_dimension=0, tiled=True
        ).astype(jnp.float32),
        lax.psum_scatter(
            up_part.astype(jnp.bfloat16), "dp", scatter_dimension=0, tiled=True
        ).astype(jnp.float32),
        lax.psum_scatter(
            down_part.astype(jnp.bfloat16), "dp", scatter_dimension=1, tiled=True
        ).astype(jnp.float32),
    )
    d_pre, grad_gain_pre_ff = norm_back(mid_rows, gain_pre_ff, d_mlp_input)
    d_mid = grad_top + d_pre
    d_attn_f, grad_gain_post_attn = norm_back(attn_proj, gain_post_attn, d_mid)
    d_attn_all = lax.all_gather(d_attn_f.astype(jnp.bfloat16), "tensor", axis=0, tiled=True)
    out_part = contract_rows(context_b, d_attn_all)
    d_context = (
        project_back(d_attn_all, out_full).astype(jnp.bfloat16).reshape(seq_rows, heads_here, HD)
    )

    def attend_back(carry, inputs):
        d_key_acc, d_value_acc = carry
        first_row, log_rows = inputs
        scores, query_blk, key_blk, value_blk, key_start = block_scores(first_row)
        attn_probs = jnp.exp(scores - log_rows[..., None])
        probs_b = attn_probs.astype(jnp.bfloat16)
        d_context_blk = lax.dynamic_slice_in_dim(d_context, first_row, q_block, 0)
        d_probs = jnp.einsum(
            "qhd,kd->hqk", d_context_blk, value_blk, preferred_element_type=jnp.float32
        )
        d_value_blk = jnp.einsum(
            "hqk,qhd->kd", probs_b, d_context_blk, preferred_element_type=jnp.float32
        )
        row_inner = jnp.sum(attn_probs * d_probs, axis=-1, keepdims=True)
        d_scores = (attn_probs * (d_probs - row_inner)).astype(jnp.bfloat16)
        d_query_blk = (
            jnp.einsum("hqk,kd->qhd", d_scores, key_blk, preferred_element_type=jnp.float32)
            * score_scale
        )
        d_key_blk = (
            jnp.einsum("hqk,qhd->kd", d_scores, query_blk, preferred_element_type=jnp.float32)
            * score_scale
        )
        d_key_acc = d_key_acc + d_key_blk
        d_value_acc = d_value_acc + d_value_blk
        return ((d_key_acc, d_value_acc), d_query_blk)

    zero_rows = jnp.zeros((seq_rows, HD), jnp.float32)
    (d_keys, d_values), d_queries = lax.scan(
        attend_back, (zero_rows, zero_rows), (starts, log_total)
    )
    d_queries = d_queries.reshape(seq_rows, heads_here, HD)

    def query_prepare(raw_rows, gain_row):
        return prepare(raw_rows, gain_row, cos_heads, sin_heads)

    def key_prepare(raw_rows, gain_row):
        return prepare(raw_rows, gain_row, cos_rows, sin_rows)

    _, query_back = jax.vjp(query_prepare, query_raw, gain_query)
    d_query_f, gain_query_part = query_back(d_queries)
    _, key_back = jax.vjp(key_prepare, key_raw, gain_key)
    d_key_f, gain_key_part = key_back(d_keys)
    d_query_b = d_query_f.reshape(seq_rows, heads_here * HD).astype(jnp.bfloat16)
    d_keyval_part = jnp.concatenate([d_key_f, d_values], axis=1)
    summed_back = lax.psum_scatter(
        jnp.concatenate([project_back(d_query_b, query_full), d_keyval_part], axis=1).astype(
            jnp.bfloat16
        ),
        "tensor",
        scatter_dimension=0,
        tiled=True,
    ).astype(jnp.float32)
    d_keyval_b = summed_back[:, model_width:].astype(jnp.bfloat16)
    d_attn_input = summed_back[:, :model_width] + project_back(d_keyval_b, keyval_full)
    query_part = contract_rows(attn_input, d_query_b)
    keyval_part = contract_rows(attn_local, d_keyval_b)
    d_in, gain_in_part = norm_back(x_local, gain_in, d_attn_input)
    grad_x = d_mid + d_in
    grad_query, grad_out = (
        lax.psum_scatter(
            query_part.astype(jnp.bfloat16), "dp", scatter_dimension=0, tiled=True
        ).astype(jnp.float32),
        lax.psum_scatter(
            out_part.astype(jnp.bfloat16), "dp", scatter_dimension=1, tiled=True
        ).astype(jnp.float32),
    )
    shared = lax.psum(
        (
            keyval_part,
            gain_in_part,
            grad_gain_post_attn,
            grad_gain_pre_ff,
            grad_gain_post_ff,
            gain_query_part,
            gain_key_part,
        ),
        ("dp", "tensor"),
    )
    shard_rows = keyval_part.shape[0] // lax.axis_size("dp")
    grad_keyval = lax.dynamic_slice_in_dim(
        shared[0], lax.axis_index("dp") * shard_rows, shard_rows, 0
    )
    return (
        output,
        grad_x,
        grad_query,
        grad_keyval,
        grad_out,
        grad_gate,
        grad_up,
        grad_down,
        shared[1],
        shared[2],
        shared[3],
        shared[4],
        shared[5],
        shared[6],
    )


def solution(mesh):
    return jax.shard_map(
        per_device,
        mesh=mesh,
        in_specs=(
            P(("dp", "tensor"), None),
            P("dp", None),
            P(("dp", "tensor"), None),
            P("dp", "tensor"),
            P("dp", None),
            P("tensor", "dp"),
            P("dp", "tensor"),
            P("dp", "tensor"),
            P("tensor", "dp"),
            P(),
            P(),
            P(),
            P(),
            P(),
            P(),
        ),
        out_specs=(
            P(("dp", "tensor"), None),
            P(("dp", "tensor"), None),
            P("dp", "tensor"),
            P("dp", None),
            P("tensor", "dp"),
            P("dp", "tensor"),
            P("dp", "tensor"),
            P("tensor", "dp"),
            P(),
            P(),
            P(),
            P(),
            P(),
            P(),
        ),
        check_vma=False,
    )
```

profile of v0, /device:TPU:1, one launch (start us, length us, event | category | flops | bytes accessed | tf_op | source)
XLA Modules:
  0.0 1217.1 jit_solution(458349446832109344)
XLA Ops:
  10.3 88.9 %all-gather.1 = bf16[32,20,512]{2,1,0:T(8,128)(2,1)S(1)} all-gather(bf16[1,20,512]{2,1,0:T(8,128)(2,1)} %bitcast.278), channel_id=1, replica_groups=mesh['dp'=32,'tensor'=4] {'dp'}, dimensions={0}, use_global_device_ids=true | all-gather | bytes 675840 | tf_op jit(solution)/shard_map/all_gather | solution.py:100
  99.4 75.5 %all-gather = bf16[32,20,256]{2,1,0:T(8,128)(2,1)S(1)} all-gather(bf16[1,20,256]{2,1,0:T(8,128)(2,1)S(1)} %bitcast.282), channel_id=1, replica_groups=mesh['dp'=32,'tensor'=4] {'dp'}, dimensions={0}, use_global_device_ids=true | all-gather | bytes 337920 | tf_op jit(solution)/shard_map/all_gather | solution.py:99
  176.6 77.2 %all-gather.2 = bf16[32,20,256]{2,1,0:T(8,128)(2,1)S(1)} all-gather(bf16[1,20,256]{2,1,0:T(8,128)(2,1)S(1)} %bitcast.283), channel_id=1, replica_groups=mesh['dp'=32,'tensor'=4] {'dp'}, dimensions={0}, use_global_device_ids=true | all-gather | bytes 337920 | tf_op jit(solution)/shard_map/all_gather | solution.py:101
  261.3 5.5 fusion.60
  270.3 14.0 %while.33 = (s32[]{:T(128)}, bf16[2,512,1,256]{3,1,2,0:T(8,128)(2,1)S(1)}, f32[2,1,512]{2,1,0:T(1,128)S(1)}, s32[2]{0:T(128)S(1)}, s32[1024]{0:T(1024)S(1)}, /*i...) while((s32[]{:T(128)}, ...), condition=%wide.region_8.9_spmd.clone, body=%wide.region_5.8_spmd.sunk.clone | while | flops 544211968 | bytes 8169671 | solution.py:139
  286.6 68.8 %reduce-scatter.15.cloned.1.call-done = f32[256,640]{1,0:T(8,128)} async-done(((f32[1024,640]{1,0:T(8,128)}), f32[256,640]{1,0:T(8,128)}) %reduce-scatter.15.cloned.1.call-update) | async-done | bytes 655376 | tf_op jit(solution)/shard_map/reduce_scatter | solution.py:142
  358.9 85.7 %all-gather.3 = bf16[32,20,512]{2,1,0:T(8,128)(2,1)S(1)} all-gather(bf16[1,20,512]{2,1,0:T(8,128)(2,1)S(1)} %bitcast.279), channel_id=1, replica_groups=mesh['dp'=32,'tensor'=4] {'dp'}, dimensions={0}, use_global_device_ids=true | all-gather | bytes 675840 | tf_op jit(solution)/shard_map/all_gather | solution.py:151
  444.8 77.7 %all-gather.4 = bf16[32,20,512]{2,1,0:T(8,128)(2,1)S(1)} all-gather(bf16[1,20,512]{2,1,0:T(8,128)(2,1)S(1)} %bitcast.280), channel_id=1, replica_groups=mesh['dp'=32,'tensor'=4] {'dp'}, dimensions={0}, use_global_device_ids=true | all-gather | bytes 675840 | tf_op jit(solution)/shard_map/all_gather | solution.py:152
  523.5 80.3 %all-gather.5 = bf16[32,20,512]{2,1,0:T(8,128)(2,1)S(1)} all-gather(bf16[1,20,512]{2,1,0:T(8,128)(2,1)S(1)} %bitcast.281), channel_id=1, replica_groups=mesh['dp'=32,'tensor'=4] {'dp'}, dimensions={0}, use_global_device_ids=true | all-gather | bytes 675840 | tf_op jit(solution)/shard_map/all_gather | solution.py:153
  613.5 67.7 %reduce-scatter.17.cloned.1.call-done = f32[256,640]{1,0:T(8,128)} async-done(((f32[1024,640]{1,0:T(8,128)}), f32[256,640]{1,0:T(8,128)}) %reduce-scatter.17.cloned.1.call-update) | async-done | bytes 655376 | tf_op jit(solution)/shard_map/reduce_scatter | solution.py:160
  685.0 11.4 reduce-scatter.19.cloned.1.call-start
  696.3 12.5 %all-gather.15.cloned.1.call-done = bf16[1024,640]{1,0:T(8,128)(2,1)} async-done(((bf16[256,640]{1,0:T(8,128)(2,1)}), bf16[1024,640]{1,0:T(8,128)(2,1)}) %all-gather.15.cloned.1.call-update) | async-done | bytes 1310736 | tf_op jit(solution)/shard_map/all_gather | solution.py:169
  708.9 5.2 multiply_convert_fusion
  718.3 33.4 %reduce-scatter.19.cloned.1.call-done = f32[256,640]{1,0:T(8,128)} async-done(((f32[1024,640]{1,0:T(8,128)}), f32[256,640]{1,0:T(8,128)}) %reduce-scatter.19.cloned.1.call-update) | async-done | bytes 655376 | tf_op jit(solution)/shard_map/reduce_scatter | solution.py:178
  755.5 23.8 %all-gather.17.cloned.1.call-done = bf16[1024,640]{1,0:T(8,128)(2,1)} async-done(((bf16[256,640]{1,0:T(8,128)(2,1)}), bf16[1024,640]{1,0:T(8,128)(2,1)}) %all-gather.17.cloned.1.call-update) | async-done | bytes 1310736 | tf_op jit(solution)/shard_map/all_gather | solution.py:198
  782.1 36.4 %while.34 = (s32[]{:T(128)}, f32[1024,256]{1,0:T(8,128)}, f32[1024,256]{1,0:T(8,128)}, f32[2,512,1,256]{3,1,2,0:T(8,128)}, s32[2]{0:T(128)S(1)}, /*index=5*/s32[...) while((s32[]{:T(128)}, f32[1024,256]{1,0:T(8,128)}, ...), condition=%wide.region_20.21_spmd.clone.clone, body=%wide.region_18.20_spmd.clone.sunk.clone | while | flops 1351484416 | bytes 46170532 | solution.py:232
  850.3 103.2 %fusion.97 = (bf16[24,256]{1,0:T(8,128)(2,1)S(1)}, bf16[256,24]{0,1:T(8,128)(2,1)S(1)}, bf16[24,512]{1,0:T(8,128)(2,1)S(1)}, bf16[24,512]{1,0:T(8,128)(2,1)S(1)}, bf16[512,24]{0,1:T(8,128)(2,1)S(1)}) fusion(bf16[640,256]{1,0:T(8,128)(2,1)S(1)} %convolution_convert_fusion.6, bf16[256,640]{0,1:T(8,128)(2,1)S(1)} %convolution_convert_fusion.5, ...), kind=kCustom, calls=%all-reduce-scatter.5 | all-reduce-scatter fusion | flops 1572865 | bytes 2720256
  956.1 5.0 collective-permute-start.17
  969.2 6.3 collective-permute-start.6
  981.0 5.3 collective-permute-start.9
  991.9 4.9 collective-permute-start.2
  1002.6 5.2 collective-permute-start.25
  1047.7 82.1 %all-reduce.14 = (f32[640]{0:T(1024)}, f32[640]{0:T(1024)}, f32[640]{0:T(1024)}, f32[640]{0:T(1024)}, f32[256]{0:T(256)}, /*index=5*/f32[256]{0:T(256)}) all-reduce(f32[640]{0:T(1024)S(1)} %get-tuple-element.396, f32[640]{0:T(1024)S(1)} %get-tuple-element.392, ...), channel_id=1, replica_groups=mesh['dp'=32,'tensor'=4] {'dp','tensor'}, use_global_device_ids=true, to_apply=%region_32.33 | all-reduce | flops 3072 | bytes 24576 | tf_op jit(solution)/shard_map/psum | solution.py:271
  1130.8 77.9 %all-reduce.18.cloned.1.call-done = f32[640,512]{1,0:T(8,128)} async-done(((f32[640,512]{1,0:T(8,128)}), f32[640,512]{1,0:T(8,128)}) %all-reduce.18.cloned.1.call-update) | async-done | bytes 1310736 | tf_op jit(solution)/shard_map/psum | solution.py:271
  (350 shorter events, 186.2 us)
Async XLA Ops:
  7.2 247.9 %all-gather.11.cloned.1.call-start = ((), (), s32[]{:S(2)}) async-start(), calls=%async_computation.4 | async-start | bytes 1638400 | tf_op jit(solution)/shard_map/all_gather | solution.py:103
  10.3 345.1 %reduce-scatter.15.cloned.1.call-start = ((), (), s32[]{:S(2)}) async-start(), calls=%async_computation.5 | async-start | bytes 3276800 | tf_op jit(solution)/shard_map/reduce_scatter | solution.py:142
  286.5 318.3 %all-gather.13.cloned.1.call-start = ((), (), s32[]{:S(2)}) async-start(), calls=%async_computation.6 | async-start | bytes 1638400 | tf_op jit(solution)/shard_map/all_gather | solution.py:155
  358.9 322.3 %reduce-scatter.17.cloned.1.call-start = ((), (), s32[]{:S(2)}) async-start(), calls=%async_computation.7 | async-start | bytes 3276800 | tf_op jit(solution)/shard_map/reduce_scatter | solution.py:160
  613.4 95.4 %all-gather.15.cloned.1.call-start = ((), (), s32[]{:S(2)}) async-start(), calls=%async_computation.8 | async-start | bytes 1638400 | tf_op jit(solution)/shard_map/all_gather | solution.py:169
  685.0 66.7 %reduce-scatter.19.cloned.1.call-start = ((), (), s32[]{:S(2)}) async-start(), calls=%async_computation.9 | async-start | bytes 3276800 | tf_op jit(solution)/shard_map/reduce_scatter | solution.py:178
  718.2 61.1 %all-gather.17.cloned.1.call-start = ((), (), s32[]{:S(2)}) async-start(), calls=%async_computation.10 | async-start | bytes 1638400 | tf_op jit(solution)/shard_map/all_gather | solution.py:198
  755.4 288.2 %reduce-scatter.21.cloned.1.call-start = ((), (), s32[]{:S(2)}) async-start(), calls=%async_computation.11 | async-start | bytes 2949120 | tf_op jit(solution)/shard_map/reduce_scatter | solution.py:249
  842.1 366.7 %all-reduce.18.cloned.1.call-start = ((), (), s32[]{:S(2)}) async-start(), calls=%async_computation.12 | async-start | bytes 2621440 | tf_op jit(solution)/shard_map/psum | solution.py:271
  953.5 22.0 %collective-permute-start.29 = (bf16[512,4]{0,1:T(4,128)(2,1)S(1)}, bf16[512,4]{0,1:T(4,128)(2,1)S(1)}, u32[]{:S(2)}, u32[]{:S(2)}) collective-permute-start(bf16[512,4]{0,1:T(4,128)(2,1)S(1)} %slice.73), channel_id=1, source_target_pairs={{0,24},{4,28},{8,32},{12,36},{16,40},{20,44},{24,48},{28,52},{32,5... | collective-permute-start | bytes 12296
  954.8 23.8 %collective-permute-start.23 = (bf16[4,512]{1,0:T(4,128)(2,1)S(1)}, bf16[4,512]{1,0:T(4,128)(2,1)S(1)}, u32[]{:S(2)}, u32[]{:S(2)}) collective-permute-start(bf16[4,512]{1,0:T(4,128)(2,1)S(1)} %slice.72), channel_id=1, source_target_pairs={{0,24},{4,28},{8,32},{12,36},{16,40},{20,44},{24,48},{28,52},{32,5... | collective-permute-start | bytes 12296
  956.1 24.8 %collective-permute-start.17 = (bf16[4,512]{1,0:T(4,128)(2,1)S(1)}, bf16[4,512]{1,0:T(4,128)(2,1)S(1)}, u32[]{:S(2)}, u32[]{:S(2)}) collective-permute-start(bf16[4,512]{1,0:T(4,128)(2,1)S(1)} %slice.71), channel_id=1, source_target_pairs={{0,24},{4,28},{8,32},{12,36},{16,40},{20,44},{24,48},{28,52},{32,5... | collective-permute-start | bytes 12296
  967.9 18.4 %collective-permute-start.10 = (bf16[256,24]{0,1:T(8,128)(2,1)S(1)}, bf16[256,24]{0,1:T(8,128)(2,1)S(1)}, u32[]{:S(2)}, u32[]{:S(2)}) collective-permute-start(bf16[256,24]{0,1:T(8,128)(2,1)S(1)} %get-tuple-element.452), channel_id=1, source_target_pairs={{0,20},{4,24},{8,28},{12,32},{16,36},{20,40},{24,44},{28,48},{32,5... | collective-permute-start | bytes 36872
  969.2 20.2 %collective-permute-start.6 = (bf16[256,24]{0,1:T(8,128)(2,1)S(1)}, bf16[256,24]{0,1:T(8,128)(2,1)S(1)}, u32[]{:S(2)}, u32[]{:S(2)}) collective-permute-start(bf16[256,24]{0,1:T(8,128)(2,1)S(1)} %get-tuple-element.452), channel_id=1, source_target_pairs={{0,4},{4,8},{8,12},{12,16},{16,20},{20,24},{24,28},{28,32},{32,36}... | collective-permute-start | bytes 36872
  975.5 16.4 %collective-permute-start.7 = (bf16[256,24]{0,1:T(8,128)(2,1)S(1)}, bf16[256,24]{0,1:T(8,128)(2,1)S(1)}, u32[]{:S(2)}, u32[]{:S(2)}) collective-permute-start(bf16[256,24]{0,1:T(8,128)(2,1)S(1)} %get-tuple-element.452), channel_id=1, source_target_pairs={{0,8},{4,12},{8,16},{12,20},{16,24},{20,28},{24,32},{28,36},{32,40... | collective-permute-start | bytes 36872
  978.7 18.2 %collective-permute-start.8 = (bf16[256,24]{0,1:T(8,128)(2,1)S(1)}, bf16[256,24]{0,1:T(8,128)(2,1)S(1)}, u32[]{:S(2)}, u32[]{:S(2)}) collective-permute-start(bf16[256,24]{0,1:T(8,128)(2,1)S(1)} %get-tuple-element.452), channel_id=1, source_target_pairs={{0,12},{4,16},{8,20},{12,24},{16,28},{20,32},{24,36},{28,40},{32,4... | collective-permute-start | bytes 36872
  981.0 17.8 %collective-permute-start.9 = (bf16[256,24]{0,1:T(8,128)(2,1)S(1)}, bf16[256,24]{0,1:T(8,128)(2,1)S(1)}, u32[]{:S(2)}, u32[]{:S(2)}) collective-permute-start(bf16[256,24]{0,1:T(8,128)(2,1)S(1)} %get-tuple-element.452), channel_id=1, source_target_pairs={{0,16},{4,20},{8,24},{12,28},{16,32},{20,36},{24,40},{28,44},{32,4... | collective-permute-start | bytes 36872
  986.3 14.7 %collective-permute-start = (bf16[24,256]{1,0:T(8,128)(2,1)S(1)}, bf16[24,256]{1,0:T(8,128)(2,1)S(1)}, u32[]{:S(2)}, u32[]{:S(2)}) collective-permute-start(bf16[24,256]{1,0:T(8,128)(2,1)S(1)} %get-tuple-element.451), channel_id=1, source_target_pairs={{0,4},{4,8},{8,12},{12,16},{16,20},{20,24},{24,28},{28,32},{32,36}... | collective-permute-start | bytes 36872
  991.9 16.0 %collective-permute-start.2 = (bf16[24,256]{1,0:T(8,128)(2,1)S(1)}, bf16[24,256]{1,0:T(8,128)(2,1)S(1)}, u32[]{:S(2)}, u32[]{:S(2)}) collective-permute-start(bf16[24,256]{1,0:T(8,128)(2,1)S(1)} %get-tuple-element.451), channel_id=1, source_target_pairs={{0,12},{4,16},{8,20},{12,24},{16,28},{20,32},{24,36},{28,40},{32,4... | collective-permute-start | bytes 36872
  1001.0 13.6 %collective-permute-start.24 = (bf16[512,24]{0,1:T(8,128)(2,1)S(1)}, bf16[512,24]{0,1:T(8,128)(2,1)S(1)}, u32[]{:S(2)}, u32[]{:S(2)}) collective-permute-start(bf16[512,24]{0,1:T(8,128)(2,1)S(1)} %get-tuple-element.455), channel_id=1, source_target_pairs={{0,4},{4,8},{8,12},{12,16},{16,20},{20,24},{24,28},{28,32},{32,36}... | collective-permute-start | bytes 73736
  1002.6 14.2 %collective-permute-start.25 = (bf16[512,24]{0,1:T(8,128)(2,1)S(1)}, bf16[512,24]{0,1:T(8,128)(2,1)S(1)}, u32[]{:S(2)}, u32[]{:S(2)}) collective-permute-start(bf16[512,24]{0,1:T(8,128)(2,1)S(1)} %get-tuple-element.455), channel_id=1, source_target_pairs={{0,8},{4,12},{8,16},{12,20},{16,24},{20,28},{24,32},{28,36},{32,40... | collective-permute-start | bytes 73736
  1007.9 13.6 %collective-permute-start.26 = (bf16[512,24]{0,1:T(8,128)(2,1)S(1)}, bf16[512,24]{0,1:T(8,128)(2,1)S(1)}, u32[]{:S(2)}, u32[]{:S(2)}) collective-permute-start(bf16[512,24]{0,1:T(8,128)(2,1)S(1)} %get-tuple-element.455), channel_id=1, source_target_pairs={{0,12},{4,16},{8,20},{12,24},{16,28},{20,32},{24,36},{28,40},{32,4... | collective-permute-start | bytes 73736
  1009.2 13.8 %collective-permute-start.27 = (bf16[512,24]{0,1:T(8,128)(2,1)S(1)}, bf16[512,24]{0,1:T(8,128)(2,1)S(1)}, u32[]{:S(2)}, u32[]{:S(2)}) collective-permute-start(bf16[512,24]{0,1:T(8,128)(2,1)S(1)} %get-tuple-element.455), channel_id=1, source_target_pairs={{0,16},{4,20},{8,24},{12,28},{16,32},{20,36},{24,40},{28,44},{32,4... | collective-permute-start | bytes 73736
  1010.8 13.5 %collective-permute-start.28 = (bf16[512,24]{0,1:T(8,128)(2,1)S(1)}, bf16[512,24]{0,1:T(8,128)(2,1)S(1)}, u32[]{:S(2)}, u32[]{:S(2)}) collective-permute-start(bf16[512,24]{0,1:T(8,128)(2,1)S(1)} %get-tuple-element.455), channel_id=1, source_target_pairs={{0,20},{4,24},{8,28},{12,32},{16,36},{20,40},{24,44},{28,48},{32,5... | collective-permute-start | bytes 73736
  (82 other events, 2184.7 us)
Sparse Core Ops, SparseCore 0:
  10.4 27.1 all-gather.10
  286.6 68.7 reduce-scatter.14
  359.0 24.7 all-gather.12
  613.5 67.5 reduce-scatter.16
  685.1 23.7 all-gather.14
  718.3 33.2 reduce-scatter.18
  755.5 23.7 all-gather.16
  842.2 35.8 reduce-scatter.20
  1046.2 162.5 all-reduce.17
where the time goes:
time: 1230 us; the launch traced here: 1220 us
  blocking collectives  670 us (54%)
  waiting for transfers between devices  284 us (23%)
  starting transfers between devices  92.6 us (8%)
  matrix products  65.9 us (5%)
  other arithmetic  48.6 us (4%)
  local copies, waits for them, and re-layouts  27.5 us (2%)
  between operations  17 us (1%)
    unnamed x1, blocking collectives  103 us
    all_gather x1, blocking collectives, per_device(): lax.all_gather(w_keyval, 'dp', axis=0, tiled=True)  88.9 us
    all_gather x1, blocking collectives, per_device(): lax.all_gather(w_gate, 'dp', axis=0, tiled=True)  85.7 us
    psum x1, blocking collectives, per_device(): lax.psum((keyval_part, gain_in_part, grad_gain_post_attn, grad_gain_pre_f...  82.1 us
    unnamed x30, starting transfers between devices  80.8 us
    all_gather x1, blocking collectives, per_device(): lax.all_gather(w_down, 'dp', axis=1, tiled=True)  80.3 us
    psum x1, waiting for transfers between devices, per_device(): lax.psum((keyval_part, gain_in_part, grad_gain_post_attn, grad_gain_pre_f...  77.9 us
    all_gather x1, blocking collectives, per_device(): lax.all_gather(w_up, 'dp', axis=0, tiled=True)  77.7 us
  transfers between devices with their start and end apart: 39, of which 6 were waited for; matrix products, arithmetic and copies ran while one was open for 10% of the time, Pallas kernels for 0%

commit v1 on v0

--- a/solution.py
+++ b/solution.py
@@ -7,6 +7,11 @@
 WINDOW = 512
 norm_eps = 1e-06
 rope_base = 10000.0
+
+
+def exchange_gather(block, axis, dim):
+    stack = jnp.stack([block] * lax.axis_size(axis))
+    return jnp.concatenate(lax.all_to_all(stack, axis, 0, 0), axis=dim)
 
 
 def rms_scale(array_in, gain_row):
@@ -98,7 +103,7 @@
     query_full, keyval_full, out_full = (
         lax.all_gather(w_query, "dp", axis=0, tiled=True),
         lax.all_gather(w_keyval, "dp", axis=0, tiled=True),
-        lax.all_gather(w_out, "dp", axis=1, tiled=True),
+        exchange_gather(w_out, "dp", 1),
     )
     attn_input = lax.all_gather(attn_local, "tensor", axis=0, tiled=True)
     query_raw = jnp.dot(attn_input, query_full, preferred_element_type=jnp.float32).reshape(

time: 1230 us -> 1150 us (0.935)
  blocking collectives: 670 us -> 591 us
  starting transfers between devices: 92.6 us -> 105 us
    all_gather x1 -> x0, blocking collectives: 77.2 us -> none  [per_device(): lax.all_gather(w_out, 'dp', axis=1, tiled=True)]
  transfers between devices with their start and end apart: 39 -> 40, of which waited for: 6 -> 6; matrix products, arithmetic and copies ran while one was open for 10% -> 11% of each run, Pallas kernels for 0% -> 0%
where the time goes in v1:
time: 1150 us; the launch traced here: 1140 us
  blocking collectives  591 us (51%)
  waiting for transfers between devices  273 us (24%)
  starting transfers between devices  105 us (9%)
  matrix products  65.9 us (6%)
  other arithmetic  48.6 us (4%)
  local copies, waits for them, and re-layouts  29 us (3%)
  between operations  17 us (1%)
    unnamed x1, blocking collectives  103 us
    all_gather x1, blocking collectives, per_device(): lax.all_gather(w_keyval, 'dp', axis=0, tiled=True)  86.8 us
    all_gather x1, blocking collectives, per_device(): lax.all_gather(w_gate, 'dp', axis=0, tiled=True)  86.1 us
    psum x1, blocking collectives, per_device(): lax.psum((keyval_part, gain_in_part, grad_gain_post_attn, grad_gain_pre_f...  82 us
    unnamed x30, starting transfers between devices  80.8 us
    all_gather x1, blocking collectives, per_device(): lax.all_gather(w_down, 'dp', axis=1, tiled=True)  79 us
    all_gather x1, blocking collectives, per_device(): lax.all_gather(w_up, 'dp', axis=0, tiled=True)  78.2 us
    psum x1, waiting for transfers between devices, per_device(): lax.psum((keyval_part, gain_in_part, grad_gain_post_attn, grad_gain_pre_f...  77.9 us
  transfers between devices with their start and end apart: 40, of which 6 were waited for; matrix products, arithmetic and copies ran while one was open for 11% of the time, Pallas kernels for 0%

profile of v1, /device:TPU:1, one launch (start us, length us, event | category | flops | bytes accessed | tf_op | source)
XLA Modules:
  0.0 1139.9 jit_solution(15518354489111897827)
XLA Ops:
  11.8 11.5 %all-to-all-start = ((bf16[32,256,20]{1,2,0:T(8,128)(2,1)}), bf16[32,256,20]{1,2,0:T(8,128)(2,1)S(1)}, u32[]{:S(2)}, u32[]{:S(2)}) async-start(bf16[32,256,20]{1,2,0:T(8,128)(2,1)} %stack.2), calls=%async_computation | async-start | bytes 786432 | tf_op jit(solution)/shard_map/all_to_all | solution.py:14
  23.3 86.8 %all-gather.1 = bf16[32,20,512]{2,1,0:T(8,128)(2,1)S(1)} all-gather(bf16[1,20,512]{2,1,0:T(8,128)(2,1)S(1)} %bitcast.279), channel_id=1, replica_groups=mesh['dp'=32,'tensor'=4] {'dp'}, dimensions={0}, use_global_device_ids=true | all-gather | bytes 675840 | tf_op jit(solution)/shard_map/all_gather | solution.py:105
  110.2 75.5 %all-gather = bf16[32,20,256]{2,1,0:T(8,128)(2,1)S(1)} all-gather(bf16[1,20,256]{2,1,0:T(8,128)(2,1)S(1)} %bitcast.283), channel_id=1, replica_groups=mesh['dp'=32,'tensor'=4] {'dp'}, dimensions={0}, use_global_device_ids=true | all-gather | bytes 337920 | tf_op jit(solution)/shard_map/all_gather | solution.py:104
  195.0 5.5 fusion.60
  204.0 14.0 %while.33 = (s32[]{:T(128)}, bf16[2,512,1,256]{3,1,2,0:T(8,128)(2,1)S(1)}, f32[2,1,512]{2,1,0:T(1,128)S(1)}, s32[2]{0:T(128)S(1)}, s32[1024]{0:T(1024)S(1)}, /*i...) while((s32[]{:T(128)}, ...), condition=%wide.region_8.9_spmd.clone, body=%wide.region_5.8_spmd.sunk.clone | while | flops 544211968 | bytes 8169671 | solution.py:144
  220.3 58.0 %reduce-scatter.15.cloned.1.call-done = f32[256,640]{1,0:T(8,128)} async-done(((f32[1024,640]{1,0:T(8,128)}), f32[256,640]{1,0:T(8,128)}) %reduce-scatter.15.cloned.1.call-update) | async-done | bytes 655376 | tf_op jit(solution)/shard_map/reduce_scatter | solution.py:147
  281.9 86.1 %all-gather.2 = bf16[32,20,512]{2,1,0:T(8,128)(2,1)S(1)} all-gather(bf16[1,20,512]{2,1,0:T(8,128)(2,1)S(1)} %bitcast.280), channel_id=1, replica_groups=mesh['dp'=32,'tensor'=4] {'dp'}, dimensions={0}, use_global_device_ids=true | all-gather | bytes 675840 | tf_op jit(solution)/shard_map/all_gather | solution.py:156
  368.1 78.2 %all-gather.3 = bf16[32,20,512]{2,1,0:T(8,128)(2,1)S(1)} all-gather(bf16[1,20,512]{2,1,0:T(8,128)(2,1)S(1)} %bitcast.281), channel_id=1, replica_groups=mesh['dp'=32,'tensor'=4] {'dp'}, dimensions={0}, use_global_device_ids=true | all-gather | bytes 675840 | tf_op jit(solution)/shard_map/all_gather | solution.py:157
  447.4 79.0 %all-gather.4 = bf16[32,20,512]{2,1,0:T(8,128)(2,1)S(1)} all-gather(bf16[1,20,512]{2,1,0:T(8,128)(2,1)S(1)} %bitcast.282), channel_id=1, replica_groups=mesh['dp'=32,'tensor'=4] {'dp'}, dimensions={0}, use_global_device_ids=true | all-gather | bytes 675840 | tf_op jit(solution)/shard_map/all_gather | solution.py:158
  536.0 11.8 %all-gather.14.cloned.1.call-start = ((), (), s32[]{:S(2)}) async-start(), calls=%async_computation.9 | async-start | bytes 1638400 | tf_op jit(solution)/shard_map/all_gather | solution.py:174
  547.8 56.3 %reduce-scatter.17.cloned.1.call-done = f32[256,640]{1,0:T(8,128)} async-done(((f32[1024,640]{1,0:T(8,128)}), f32[256,640]{1,0:T(8,128)}) %reduce-scatter.17.cloned.1.call-update) | async-done | bytes 655376 | tf_op jit(solution)/shard_map/reduce_scatter | solution.py:165
  607.9 23.8 %all-gather.14.cloned.1.call-done = bf16[1024,640]{1,0:T(8,128)(2,1)} async-done(((bf16[256,640]{1,0:T(8,128)(2,1)}), bf16[1024,640]{1,0:T(8,128)(2,1)}) %all-gather.14.cloned.1.call-update) | async-done | bytes 1310736 | tf_op jit(solution)/shard_map/all_gather | solution.py:174
  631.8 5.2 multiply_convert_fusion
  641.1 33.4 %reduce-scatter.19.cloned.1.call-done = f32[256,640]{1,0:T(8,128)} async-done(((f32[1024,640]{1,0:T(8,128)}), f32[256,640]{1,0:T(8,128)}) %reduce-scatter.19.cloned.1.call-update) | async-done | bytes 655376 | tf_op jit(solution)/shard_map/reduce_scatter | solution.py:183
  678.4 23.8 %all-gather.16.cloned.1.call-done = bf16[1024,640]{1,0:T(8,128)(2,1)} async-done(((bf16[256,640]{1,0:T(8,128)(2,1)}), bf16[1024,640]{1,0:T(8,128)(2,1)}) %all-gather.16.cloned.1.call-update) | async-done | bytes 1310736 | tf_op jit(solution)/shard_map/all_gather | solution.py:203
  705.0 36.4 %while.34 = (s32[]{:T(128)}, f32[1024,256]{1,0:T(8,128)}, f32[1024,256]{1,0:T(8,128)}, f32[2,512,1,256]{3,1,2,0:T(8,128)}, s32[2]{0:T(128)S(1)}, /*index=5*/s32[...) while((s32[]{:T(128)}, f32[1024,256]{1,0:T(8,128)}, ...), condition=%wide.region_20.21_spmd.clone.clone, body=%wide.region_18.20_spmd.clone.sunk.clone | while | flops 1351484416 | bytes 46170532 | solution.py:237
  773.1 103.2 %fusion.97 = (bf16[24,256]{1,0:T(8,128)(2,1)S(1)}, bf16[256,24]{0,1:T(8,128)(2,1)S(1)}, bf16[24,512]{1,0:T(8,128)(2,1)S(1)}, bf16[24,512]{1,0:T(8,128)(2,1)S(1)}, bf16[512,24]{0,1:T(8,128)(2,1)S(1)}) fusion(bf16[640,256]{1,0:T(8,128)(2,1)S(1)} %convolution_convert_fusion.6, bf16[256,640]{0,1:T(8,128)(2,1)S(1)} %convolution_convert_fusion.5, ...), kind=kCustom, calls=%all-reduce-scatter.5 | all-reduce-scatter fusion | flops 1572865 | bytes 2720256
  878.9 4.9 collective-permute-start.17
  892.0 6.3 collective-permute-start.6
  903.8 5.3 collective-permute-start.9
  914.7 4.9 collective-permute-start.2
  925.4 5.2 collective-permute-start.25
  970.5 82.0 %all-reduce.14 = (f32[640]{0:T(1024)}, f32[640]{0:T(1024)}, f32[640]{0:T(1024)}, f32[640]{0:T(1024)}, f32[256]{0:T(256)}, /*index=5*/f32[256]{0:T(256)}) all-reduce(f32[640]{0:T(1024)S(1)} %get-tuple-element.396, f32[640]{0:T(1024)S(1)} %get-tuple-element.392, ...), channel_id=1, replica_groups=mesh['dp'=32,'tensor'=4] {'dp','tensor'}, use_global_device_ids=true, to_apply=%region_32.33 | all-reduce | flops 3072 | bytes 24576 | tf_op jit(solution)/shard_map/psum | solution.py:276
  1053.6 77.9 %all-reduce.18.cloned.1.call-done = f32[640,512]{1,0:T(8,128)} async-done(((f32[640,512]{1,0:T(8,128)}), f32[640,512]{1,0:T(8,128)}) %all-reduce.18.cloned.1.call-update) | async-done | bytes 1310736 | tf_op jit(solution)/shard_map/psum | solution.py:276
  (352 shorter events, 187.6 us)
Async XLA Ops:
  7.2 181.5 %all-gather.10.cloned.1.call-start = ((), (), s32[]{:S(2)}) async-start(), calls=%async_computation.5 | async-start | bytes 1638400 | tf_op jit(solution)/shard_map/all_gather | solution.py:108
  11.8 176.9 %all-to-all-start = ((bf16[32,256,20]{1,2,0:T(8,128)(2,1)}), bf16[32,256,20]{1,2,0:T(8,128)(2,1)S(1)}, u32[]{:S(2)}, u32[]{:S(2)}) async-start(bf16[32,256,20]{1,2,0:T(8,128)(2,1)} %stack.2), calls=%async_computation | async-start | bytes 786432 | tf_op jit(solution)/shard_map/all_to_all | solution.py:14
  23.2 255.1 %reduce-scatter.15.cloned.1.call-start = ((), (), s32[]{:S(2)}) async-start(), calls=%async_computation.6 | async-start | bytes 3276800 | tf_op jit(solution)/shard_map/reduce_scatter | solution.py:147
  220.2 307.1 %all-gather.12.cloned.1.call-start = ((), (), s32[]{:S(2)}) async-start(), calls=%async_computation.7 | async-start | bytes 1638400 | tf_op jit(solution)/shard_map/all_gather | solution.py:160
  281.8 322.3 %reduce-scatter.17.cloned.1.call-start = ((), (), s32[]{:S(2)}) async-start(), calls=%async_computation.8 | async-start | bytes 3276800 | tf_op jit(solution)/shard_map/reduce_scatter | solution.py:165
  536.0 95.8 %all-gather.14.cloned.1.call-start = ((), (), s32[]{:S(2)}) async-start(), calls=%async_computation.9 | async-start | bytes 1638400 | tf_op jit(solution)/shard_map/all_gather | solution.py:174
  607.9 66.6 %reduce-scatter.19.cloned.1.call-start = ((), (), s32[]{:S(2)}) async-start(), calls=%async_computation.10 | async-start | bytes 3276800 | tf_op jit(solution)/shard_map/reduce_scatter | solution.py:183
  641.1 61.1 %all-gather.16.cloned.1.call-start = ((), (), s32[]{:S(2)}) async-start(), calls=%async_computation.11 | async-start | bytes 1638400 | tf_op jit(solution)/shard_map/all_gather | solution.py:203
  678.3 288.2 %reduce-scatter.21.cloned.1.call-start = ((), (), s32[]{:S(2)}) async-start(), calls=%async_computation.12 | async-start | bytes 2949120 | tf_op jit(solution)/shard_map/reduce_scatter | solution.py:254
  764.9 366.7 %all-reduce.18.cloned.1.call-start = ((), (), s32[]{:S(2)}) async-start(), calls=%async_computation.13 | async-start | bytes 2621440 | tf_op jit(solution)/shard_map/psum | solution.py:276
  876.3 22.0 %collective-permute-start.29 = (bf16[512,4]{0,1:T(4,128)(2,1)S(1)}, bf16[512,4]{0,1:T(4,128)(2,1)S(1)}, u32[]{:S(2)}, u32[]{:S(2)}) collective-permute-start(bf16[512,4]{0,1:T(4,128)(2,1)S(1)} %slice.73), channel_id=1, source_target_pairs={{0,24},{4,28},{8,32},{12,36},{16,40},{20,44},{24,48},{28,52},{32,5... | collective-permute-start | bytes 12296
  877.6 23.8 %collective-permute-start.23 = (bf16[4,512]{1,0:T(4,128)(2,1)S(1)}, bf16[4,512]{1,0:T(4,128)(2,1)S(1)}, u32[]{:S(2)}, u32[]{:S(2)}) collective-permute-start(bf16[4,512]{1,0:T(4,128)(2,1)S(1)} %slice.72), channel_id=1, source_target_pairs={{0,24},{4,28},{8,32},{12,36},{16,40},{20,44},{24,48},{28,52},{32,5... | collective-permute-start | bytes 12296
  878.9 24.8 %collective-permute-start.17 = (bf16[4,512]{1,0:T(4,128)(2,1)S(1)}, bf16[4,512]{1,0:T(4,128)(2,1)S(1)}, u32[]{:S(2)}, u32[]{:S(2)}) collective-permute-start(bf16[4,512]{1,0:T(4,128)(2,1)S(1)} %slice.71), channel_id=1, source_target_pairs={{0,24},{4,28},{8,32},{12,36},{16,40},{20,44},{24,48},{28,52},{32,5... | collective-permute-start | bytes 12296
  890.7 18.4 %collective-permute-start.10 = (bf16[256,24]{0,1:T(8,128)(2,1)S(1)}, bf16[256,24]{0,1:T(8,128)(2,1)S(1)}, u32[]{:S(2)}, u32[]{:S(2)}) collective-permute-start(bf16[256,24]{0,1:T(8,128)(2,1)S(1)} %get-tuple-element.452), channel_id=1, source_target_pairs={{0,20},{4,24},{8,28},{12,32},{16,36},{20,40},{24,44},{28,48},{32,5... | collective-permute-start | bytes 36872
  892.0 20.2 %collective-permute-start.6 = (bf16[256,24]{0,1:T(8,128)(2,1)S(1)}, bf16[256,24]{0,1:T(8,128)(2,1)S(1)}, u32[]{:S(2)}, u32[]{:S(2)}) collective-permute-start(bf16[256,24]{0,1:T(8,128)(2,1)S(1)} %get-tuple-element.452), channel_id=1, source_target_pairs={{0,4},{4,8},{8,12},{12,16},{16,20},{20,24},{24,28},{28,32},{32,36}... | collective-permute-start | bytes 36872
  898.3 16.4 %collective-permute-start.7 = (bf16[256,24]{0,1:T(8,128)(2,1)S(1)}, bf16[256,24]{0,1:T(8,128)(2,1)S(1)}, u32[]{:S(2)}, u32[]{:S(2)}) collective-permute-start(bf16[256,24]{0,1:T(8,128)(2,1)S(1)} %get-tuple-element.452), channel_id=1, source_target_pairs={{0,8},{4,12},{8,16},{12,20},{16,24},{20,28},{24,32},{28,36},{32,40... | collective-permute-start | bytes 36872
  901.5 18.2 %collective-permute-start.8 = (bf16[256,24]{0,1:T(8,128)(2,1)S(1)}, bf16[256,24]{0,1:T(8,128)(2,1)S(1)}, u32[]{:S(2)}, u32[]{:S(2)}) collective-permute-start(bf16[256,24]{0,1:T(8,128)(2,1)S(1)} %get-tuple-element.452), channel_id=1, source_target_pairs={{0,12},{4,16},{8,20},{12,24},{16,28},{20,32},{24,36},{28,40},{32,4... | collective-permute-start | bytes 36872
  903.8 17.8 %collective-permute-start.9 = (bf16[256,24]{0,1:T(8,128)(2,1)S(1)}, bf16[256,24]{0,1:T(8,128)(2,1)S(1)}, u32[]{:S(2)}, u32[]{:S(2)}) collective-permute-start(bf16[256,24]{0,1:T(8,128)(2,1)S(1)} %get-tuple-element.452), channel_id=1, source_target_pairs={{0,16},{4,20},{8,24},{12,28},{16,32},{20,36},{24,40},{28,44},{32,4... | collective-permute-start | bytes 36872
  909.1 14.7 %collective-permute-start = (bf16[24,256]{1,0:T(8,128)(2,1)S(1)}, bf16[24,256]{1,0:T(8,128)(2,1)S(1)}, u32[]{:S(2)}, u32[]{:S(2)}) collective-permute-start(bf16[24,256]{1,0:T(8,128)(2,1)S(1)} %get-tuple-element.451), channel_id=1, source_target_pairs={{0,4},{4,8},{8,12},{12,16},{16,20},{20,24},{24,28},{28,32},{32,36}... | collective-permute-start | bytes 36872
  914.7 16.0 %collective-permute-start.2 = (bf16[24,256]{1,0:T(8,128)(2,1)S(1)}, bf16[24,256]{1,0:T(8,128)(2,1)S(1)}, u32[]{:S(2)}, u32[]{:S(2)}) collective-permute-start(bf16[24,256]{1,0:T(8,128)(2,1)S(1)} %get-tuple-element.451), channel_id=1, source_target_pairs={{0,12},{4,16},{8,20},{12,24},{16,28},{20,32},{24,36},{28,40},{32,4... | collective-permute-start | bytes 36872
  923.8 13.6 %collective-permute-start.24 = (bf16[512,24]{0,1:T(8,128)(2,1)S(1)}, bf16[512,24]{0,1:T(8,128)(2,1)S(1)}, u32[]{:S(2)}, u32[]{:S(2)}) collective-permute-start(bf16[512,24]{0,1:T(8,128)(2,1)S(1)} %get-tuple-element.455), channel_id=1, source_target_pairs={{0,4},{4,8},{8,12},{12,16},{16,20},{20,24},{24,28},{28,32},{32,36}... | collective-permute-start | bytes 73736
  925.4 14.2 %collective-permute-start.25 = (bf16[512,24]{0,1:T(8,128)(2,1)S(1)}, bf16[512,24]{0,1:T(8,128)(2,1)S(1)}, u32[]{:S(2)}, u32[]{:S(2)}) collective-permute-start(bf16[512,24]{0,1:T(8,128)(2,1)S(1)} %get-tuple-element.455), channel_id=1, source_target_pairs={{0,8},{4,12},{8,16},{12,20},{16,24},{20,28},{24,32},{28,36},{32,40... | collective-permute-start | bytes 73736
  930.7 13.6 %collective-permute-start.26 = (bf16[512,24]{0,1:T(8,128)(2,1)S(1)}, bf16[512,24]{0,1:T(8,128)(2,1)S(1)}, u32[]{:S(2)}, u32[]{:S(2)}) collective-permute-start(bf16[512,24]{0,1:T(8,128)(2,1)S(1)} %get-tuple-element.455), channel_id=1, source_target_pairs={{0,12},{4,16},{8,20},{12,24},{16,28},{20,32},{24,36},{28,40},{32,4... | collective-permute-start | bytes 73736
  932.0 13.8 %collective-permute-start.27 = (bf16[512,24]{0,1:T(8,128)(2,1)S(1)}, bf16[512,24]{0,1:T(8,128)(2,1)S(1)}, u32[]{:S(2)}, u32[]{:S(2)}) collective-permute-start(bf16[512,24]{0,1:T(8,128)(2,1)S(1)} %get-tuple-element.455), channel_id=1, source_target_pairs={{0,16},{4,20},{8,24},{12,28},{16,32},{20,36},{24,40},{28,44},{32,4... | collective-permute-start | bytes 73736
  (83 other events, 1866.9 us)
Sparse Core Ops, SparseCore 0:
  10.4 29.8 all-gather.9
  220.3 57.9 reduce-scatter.14
  281.9 24.7 all-gather.11
  536.1 67.9 reduce-scatter.16
  608.0 23.7 all-gather.13
  641.2 33.2 reduce-scatter.18
  678.4 23.7 all-gather.15
  765.0 35.7 reduce-scatter.20
  969.0 162.5 all-reduce.17
